TPU v7x, 32 devices: a whole 2x2x4 slice. The times are simulated.
32 devices in a mesh: group: 1, expert: 16 (over z, y, x), step: 2 (over core).
Axes of the slice: x: 2, y: 2, z: 4, core: 2. Of those that a mesh axis runs over, the one named last changes fastest.
Arguments:
- latents: float32 [2, 2048, 1536], P('step', ('group', 'expert')), may hold values from -6 to 6
- modulation: float32 [2, 6, 1536], P('group'), may hold values from -3 to 3
- shallow_routes: int32 [2, 2048, 2], P('step', ('group', 'expert')), may hold values from 0 to 3, all different within a row; in each aligned block of 128 rows (0 to 127, 128 to 255, ..., all dimensions but the last counted through in order) at most 64 rows name the same one
- deep_routes: int32 [2048, 2], P(('group', 'expert')), may hold values from 0 to 3, all different within a row; in each aligned block of 128 rows (0 to 127, 128 to 255, ...) at most 64 rows name the same one
- refresh: int32 [16], P(('group', 'expert')), may hold values from 0 to 1
- shallow_in: bfloat16 [16, 1536, 768], P('expert'), may hold values from -0.15625 to 0.15625
- shallow_out: bfloat16 [16, 768, 1536], P('expert'), may hold values from -0.109375 to 0.109375
- deep_in: bfloat16 [16, 1536, 768], P('expert'), may hold values from -0.15625 to 0.15625
- deep_out: bfloat16 [16, 768, 1536], P('expert'), may hold values from -0.109375 to 0.109375
- shallow_router: float32 [1536, 4], replicated, may hold values from -0.15625 to 0.15625
- deep_router: float32 [1536, 4], replicated, may hold values from -0.15625 to 0.15625
Outputs:
- result: bfloat16 [2, 2048, 1536], P('step', ('group', 'expert'))
Inputs may be any that keep to these rules, and one draw needn't show every extreme that they name: `shallow_routes`: within the 128 rows of one index of expert (aligned blocks), each expert is named by at most 64 rows, and by exactly 64 rows in some block; a row names two different experts. `deep_routes`: within the 128 rows of one index of expert (aligned blocks), each expert is named by at most 64 rows, and by exactly 64 rows in some block; a row names two different experts.
All inputs are finite; a program needn't handle non-finite values.
Results may differ from a plain program's by a relative error of at most 0.01.
Values may be sent and summed in bfloat16 or wider, within the bound.
A program may use at most 64 MiB of HBM per device.

v0:
```python
import jax
import jax.numpy as jnp
from jax import lax
from jax.sharding import PartitionSpec as P


def from_root(block, axis, owner):
    block = jnp.where(lax.axis_index(axis) == owner, block, jnp.zeros_like(block))
    return lax.psum(block, axis)


def modulate(hidden, shift_row, scale_row):
    average = jnp.mean(hidden, axis=-1, keepdims=True)
    centred = hidden - average
    variance = jnp.mean(centred * centred, axis=-1, keepdims=True)
    return (centred * lax.rsqrt(variance + 1e-06) * (1.0 + scale_row) + shift_row).astype(
        jnp.bfloat16
    )


def plan(normed, routes, router, capacity):
    rows_count, width = normed.shape
    experts = router.shape[1]
    logits = jnp.dot(normed.astype(jnp.float32), router, precision=lax.Precision.HIGHEST)
    hits = routes[:, :, None] == jnp.arange(experts, dtype=jnp.int32)
    chosen = jnp.sum(jnp.where(hits, logits[:, None, :], 0.0), axis=-1)
    gate_sig = jax.nn.sigmoid(chosen)
    weights = gate_sig / jnp.sum(gate_sig, axis=-1, keepdims=True)
    pair_hits = hits.reshape(rows_count * 2, experts).astype(jnp.int32)
    position = jnp.sum(pair_hits * (jnp.cumsum(pair_hits, axis=0) - 1), axis=-1).reshape(
        rows_count, 2
    )
    slot_hit = position[:, :, None] == jnp.arange(capacity, dtype=jnp.int32)
    placed = hits[:, :, :, None] & slot_hit[:, :, None, :]
    dispatch = jnp.any(placed, axis=1).reshape(rows_count, experts * capacity).astype(jnp.bfloat16)
    gathered = jnp.einsum("rs,rd->sd", dispatch, normed, preferred_element_type=jnp.float32).astype(
        jnp.bfloat16
    )
    combine_w = jnp.sum(jnp.where(placed, weights[:, :, None, None], 0.0), axis=1)
    return (gathered.reshape(experts, capacity, width), combine_w)


def spread(gathered, slices):
    experts, capacity, width = gathered.shape
    quarters = slices // experts
    return jnp.broadcast_to(gathered[:, None], (experts, quarters, capacity, width)).reshape(
        slices, capacity, width
    )


def expert_rows(piece, weight_in, weight_out):
    dims = piece.shape
    flat_rows = piece.reshape(-1, dims[-1])
    hidden = jax.nn.gelu(
        jnp.dot(flat_rows, weight_in, preferred_element_type=jnp.float32), approximate=True
    ).astype(jnp.bfloat16)
    return (
        jnp.dot(hidden, weight_out, preferred_element_type=jnp.float32)
        .astype(jnp.bfloat16)
        .reshape(dims)
    )


def combine(summed, combine_w):
    rows_count = combine_w.shape[0]
    width = summed.shape[-1]
    return jnp.dot(
        combine_w.reshape(rows_count, -1),
        summed.reshape(-1, width),
        precision=lax.Precision.HIGHEST,
        preferred_element_type=jnp.float32,
    )


def finish(returned, combine_w):
    experts = combine_w.shape[1]
    width = returned.shape[2]
    summed = jnp.sum(
        returned.astype(jnp.float32).reshape(experts, -1, returned.shape[1], width), axis=1
    )
    return combine(summed, combine_w)


def body(
    latents,
    modulation,
    shallow_routes,
    deep_routes,
    refresh,
    shallow_in,
    shallow_out,
    deep_in,
    deep_out,
    shallow_router,
    deep_router,
):
    slices = lax.axis_size("expert")
    experts = shallow_router.shape[1]
    rows_count = latents.shape[1]
    capacity = 2 * max(rows_count * 5 // 64, rows_count // experts)
    step_idx = lax.axis_index("step")
    root_idx = refresh[0]
    own_mod = lax.dynamic_index_in_dim(modulation, step_idx, 0, keepdims=False)
    features = latents[0]
    normed = modulate(features, own_mod[0], own_mod[1])
    gathered, combine_w = plan(normed, shallow_routes[0], shallow_router, capacity)
    partial_value = expert_rows(
        lax.all_to_all(spread(gathered, slices), "expert", split_axis=0, concat_axis=0, tiled=True),
        shallow_in[0],
        shallow_out[0],
    )
    returned = lax.all_to_all(partial_value, "expert", split_axis=0, concat_axis=0, tiled=True)
    moe_shallow = finish(returned, combine_w)
    after_shallow = (features + own_mod[2] * moe_shallow).astype(jnp.bfloat16)
    normed_deep = modulate(after_shallow.astype(jnp.float32), own_mod[3], own_mod[4])
    gathered_deep, combine_deep = plan(normed_deep, deep_routes, deep_router, capacity)
    partial_value = expert_rows(
        lax.all_to_all(
            spread(gathered_deep, slices), "expert", split_axis=0, concat_axis=0, tiled=True
        ),
        deep_in[0],
        deep_out[0],
    )
    returned_deep = lax.all_to_all(partial_value, "expert", split_axis=0, concat_axis=0, tiled=True)
    moe_deep = finish(returned_deep, combine_deep)
    own_delta = (own_mod[5] * moe_deep).astype(jnp.bfloat16)
    deep_delta = from_root(own_delta, "step", root_idx)
    result = (after_shallow.astype(jnp.float32) + deep_delta.astype(jnp.float32)).astype(
        jnp.bfloat16
    )
    return result[None]


def solution(mesh):
    in_specs = (
        P("step", ("group", "expert"), None),
        P("group", None, None),
        P("step", ("group", "expert"), None),
        P(("group", "expert"), None),
        P(("group", "expert")),
        P("expert", None, None),
        P("expert", None, None),
        P("expert", None, None),
        P("expert", None, None),
        P(),
        P(),
    )
    out_specs = P("step", ("group", "expert"), None)
    return jax.shard_map(body, mesh=mesh, in_specs=in_specs, out_specs=out_specs, check_vma=False)
```

profile of v0, /device:TPU:0, one launch (start us, length us, event | category | flops | bytes accessed | tf_op | source)
XLA Modules:
  0.0 376.1 jit_solution(6678324923360058093)
XLA Ops:
  6.5 0.0 copy-start
  6.5 0.9 copy.32
  7.5 0.1 eq.123
  7.6 0.1 eq.119
  7.8 1.3 reduce_sum.127
  9.0 1.4 multiply_reduce_fusion.1
  10.4 0.7 iota_compare_fusion.5
  11.1 1.2 reduce-window.14
  12.3 0.1 slice.46
  12.4 0.1 copy.34
  12.5 0.1 copy.35
  12.6 0.1 add_bitcast_fusion.1
  12.7 0.1 eq.127
  12.9 0.1 copy.36
  13.0 0.9 dynamic-slice_reduce_fusion.1
  13.9 1.6 convolution_convert_fusion.3
  15.6 0.3 broadcast_in_dim.82
  15.9 79.5 %all_to_all.20 = bf16[16,64,1536]{2,1,0:T(8,128)(2,1)} all-to-all(bf16[16,64,1536]{2,1,0:T(8,128)(2,1)S(1)} %bitcast.112), channel_id=1, replica_groups=mesh['group'=1,'expert'=16,'step'=2] {'expert'}, dimensions={0} | all-to-all | bytes 6291456 | tf_op jit(solution)/shard_map/all_to_all | solution.py:108
  95.4 0.0 copy-done
  95.4 10.4 %convolution_convert_fusion.1 = bf16[1024,1536]{1,0:T(8,128)(2,1)} fusion(bf16[1,768,1536]{2,1,0:T(8,128)(2,1)S(1)} %copy-done, bf16[1024,1536]{1,0:T(8,128)(2,1)} %bitcast.116, bf16[1,1536,768]{2,1,0:T(8,128)(2,1)} %param.16), kind=kOutput, calls=%fused_computation.5 | convolution fusion | flops 4840488960 | bytes 11010048 | tf_op jit(solution)/shard_map/dot_general | solution.py:58
  105.8 0.0 copy-start.1
  105.8 0.0 copy-start.4
  105.8 0.0 copy-start.6
  105.8 4.6 %all-to-all-start.1 = ((bf16[16,64,1536]{2,1,0:T(8,128)(2,1)}), bf16[16,64,1536]{2,1,0:T(8,128)(2,1)}, u32[]{:S(2)}, u32[]{:S(2)}) async-start(bf16[16,64,1536]{2,1,0:T(8,128)(2,1)} %bitcast.114), calls=%async_computation.1 | async-start | bytes 6291456 | tf_op jit(solution)/shard_map/all_to_all | solution.py:112
  110.5 0.0 copy-done.7
  110.5 0.1 copy.37
  110.6 0.1 eq.139
  110.8 0.1 eq.135
  110.9 1.2 reduce-window.16
  112.1 0.1 slice.47
  112.2 0.1 copy.39
  112.4 0.1 copy.40
  112.4 0.1 add_bitcast_fusion
  112.5 0.1 eq.143
  112.7 0.1 copy.41
  112.8 0.0 copy-done.1
  112.8 0.0 copy-done.4
  112.8 0.5 fusion.44
  113.3 0.0 copy-done.6
  113.5 57.2 %all-to-all-done.1 = bf16[16,64,1536]{2,1,0:T(8,128)(2,1)} async-done(((bf16[16,64,1536]{2,1,0:T(8,128)(2,1)}), bf16[16,64,1536]{2,1,0:T(8,128)(2,1)}, u32[]{:S(2)}, u32[]{:S(2)}) %all-to-all-start.1) | async-done | bytes 3145760 | tf_op jit(solution)/shard_map/all_to_all | solution.py:112
  170.7 2.6 convert_reduce_fusion.1
  173.2 1.1 fusion.61
  174.3 0.0 copy-start.2
  174.3 0.2 multiply_reduce_fusion
  174.6 0.2 add_convert_fusion.1
  174.8 0.3 convolution_convert_fusion.2
  175.1 0.1 copy-done.2
  175.2 0.3 broadcast_in_dim.86
  175.5 84.7 %all_to_all.21 = bf16[16,64,1536]{2,1,0:T(8,128)(2,1)} all-to-all(bf16[16,64,1536]{2,1,0:T(8,128)(2,1)S(1)} %bitcast.113), channel_id=1, replica_groups=mesh['group'=1,'expert'=16,'step'=2] {'expert'}, dimensions={0} | all-to-all | bytes 6291456 | tf_op jit(solution)/shard_map/all_to_all | solution.py:118
  260.2 11.1 %convolution_convert_fusion = bf16[1024,1536]{1,0:T(8,128)(2,1)} fusion(bf16[1,768,1536]{2,1,0:T(8,128)(2,1)} %param.19, bf16[1024,1536]{1,0:T(8,128)(2,1)} %bitcast.117, bf16[1,1536,768]{2,1,0:T(8,128)(2,1)} %param.18), kind=kOutput, calls=%fused_computation.4 | convolution fusion | flops 4840488960 | bytes 11010048 | tf_op jit(solution)/shard_map/dot_general | solution.py:58
  271.3 0.0 copy-start.5
  271.3 4.6 %all-to-all-start.3 = ((bf16[16,64,1536]{2,1,0:T(8,128)(2,1)}), bf16[16,64,1536]{2,1,0:T(8,128)(2,1)}, u32[]{:S(2)}, u32[]{:S(2)}) async-start(bf16[16,64,1536]{2,1,0:T(8,128)(2,1)} %bitcast.115), calls=%async_computation.3 | async-start | bytes 6291456 | tf_op jit(solution)/shard_map/all_to_all | solution.py:124
  275.9 0.0 all-reduce.2.cloned.1.call-start
  276.6 0.0 copy-done.5
  276.6 0.4 fusion.62
  277.1 0.1 fusion.46
  277.2 0.0 copy-start.3
  277.2 58.9 %all-to-all-done.3 = bf16[16,64,1536]{2,1,0:T(8,128)(2,1)} async-done(((bf16[16,64,1536]{2,1,0:T(8,128)(2,1)}), bf16[16,64,1536]{2,1,0:T(8,128)(2,1)}, u32[]{:S(2)}, u32[]{:S(2)}) %all-to-all-start.3) | async-done | bytes 3145760 | tf_op jit(solution)/shard_map/all_to_all | solution.py:124
  336.0 2.6 convert_reduce_fusion
  338.6 1.7 fusion.22
  340.3 0.0 all-reduce.2.cloned.1.call-update
  340.4 27.1 %all-reduce.2.cloned.1.call-done = bf16[128,1536]{1,0:T(8,128)(2,1)} async-done(((bf16[128,1536]{1,0:T(8,128)(2,1)}), bf16[128,1536]{1,0:T(8,128)(2,1)}) %all-reduce.2.cloned.1.call-update) | async-done | bytes 393232 | tf_op jit(solution)/shard_map/psum | solution.py:9
  367.4 0.0 copy-done.3
  367.4 1.8 fusion.39
  (25 shorter events, 0.5 us)
Async XLA Ops:
  6.5 88.9 %copy-start = (bf16[1,768,1536]{2,1,0:T(8,128)(2,1)S(1)}, bf16[1,768,1536]{2,1,0:T(8,128)(2,1)}, u32[]{:S(2)}) copy-start(bf16[1,768,1536]{2,1,0:T(8,128)(2,1)} %param.17) | copy-start | bytes 7077892
  105.8 4.7 %copy-start.7 = (s32[128,2]{0,1:T(2,128)S(1)}, s32[128,2]{0,1:T(2,128)}, u32[]{:S(2)}) copy-start(s32[128,2]{0,1:T(2,128)} %param.14) | copy-start | bytes 3076
  105.8 6.9 %copy-start.1 = (f32[1,128,1536]{2,1,0:T(8,128)S(1)}, f32[1,128,1536]{2,1,0:T(8,128)}, u32[]{:S(2)}) copy-start(f32[1,128,1536]{2,1,0:T(8,128)} %param.11) | copy-start | bytes 2359300
  105.8 6.9 %copy-start.4 = (f32[1536,4]{0,1:T(4,128)S(1)}, f32[1536,4]{0,1:T(4,128)}, u32[]{:S(2)}) copy-start(f32[1536,4]{0,1:T(4,128)} %param.20) | copy-start | bytes 73732
  105.8 7.4 %copy-start.6 = (s32[1,128,2]{1,2,0:T(2,128)S(1)}, s32[1,128,2]{1,2,0:T(2,128)}, u32[]{:S(2)}) copy-start(s32[1,128,2]{1,2,0:T(2,128)} %param.13) | copy-start | bytes 3076
  105.8 64.8 %all-to-all-start.1 = ((bf16[16,64,1536]{2,1,0:T(8,128)(2,1)}), bf16[16,64,1536]{2,1,0:T(8,128)(2,1)}, u32[]{:S(2)}, u32[]{:S(2)}) async-start(bf16[16,64,1536]{2,1,0:T(8,128)(2,1)} %bitcast.114), calls=%async_computation.1 | async-start | bytes 6291456 | tf_op jit(solution)/shard_map/all_to_all | solution.py:112
  174.3 0.9 copy-start.2
  271.3 5.3 %copy-start.5 = (f32[1536,4]{0,1:T(4,128)S(1)}, f32[1536,4]{0,1:T(4,128)}, u32[]{:S(2)}) copy-start(f32[1536,4]{0,1:T(4,128)} %param.21) | copy-start | bytes 73732
  271.3 64.7 %all-to-all-start.3 = ((bf16[16,64,1536]{2,1,0:T(8,128)(2,1)}), bf16[16,64,1536]{2,1,0:T(8,128)(2,1)}, u32[]{:S(2)}, u32[]{:S(2)}) async-start(bf16[16,64,1536]{2,1,0:T(8,128)(2,1)} %bitcast.115), calls=%async_computation.3 | async-start | bytes 6291456 | tf_op jit(solution)/shard_map/all_to_all | solution.py:124
  275.9 91.5 %all-reduce.2.cloned.1.call-start = ((), (), s32[]{:S(2)}) async-start(), calls=%async_computation.4 | async-start | bytes 786432 | tf_op jit(solution)/shard_map/psum | solution.py:9
  277.2 90.2 %copy-start.3 = (f32[128,1536]{1,0:T(8,128)S(1)}, f32[128,1536]{1,0:T(8,128)}, u32[]{:S(2)}) copy-start(f32[128,1536]{1,0:T(8,128)} %copy-done.2) | copy-start | bytes 2359300
Sparse Core Ops, SparseCore 0:
  340.5 26.8 all-reduce.1
where the time goes:
time: 377 us; the launch traced here: 376 us
  blocking collectives  164 us (44%)
  waiting for transfers between devices  143 us (38%)
  matrix products  27.2 us (7%)
  other arithmetic  14.7 us (4%)
  between operations  14.3 us (4%)
  starting transfers between devices  9.3 us (2%)
    all_to_all x2, waiting for transfers between devices, body(): lax.all_to_all(partial_value, 'expert', split_axis=0, concat_axis=0, tile...  116 us
    all_to_all x1, blocking collectives, body(): lax.all_to_all(spread(gathered_deep, slices), 'expert', split_axis=0, con...  84.7 us
    all_to_all x1, blocking collectives, body(): lax.all_to_all(spread(gathered, slices), 'expert', split_axis=0, concat_a...  79.5 us
    psum x1, waiting for transfers between devices, from_root(): return lax.psum(block, axis)  27.1 us
    dot_general x2, matrix products, expert_rows(): jnp.dot(hidden, weight_out, preferred_element_type=jnp.float32)  21.5 us
    all_to_all x2, starting transfers between devices, body(): lax.all_to_all(partial_value, 'expert', split_axis=0, concat_axis=0, tile...  9.25 us
  transfers between devices with their start and end apart: 3, of which 3 were waited for; matrix products, arithmetic and copies ran while one was open for 1% of the time, Pallas kernels for 0%

commit v1 on v0

v1 whole, which is shorter than its diff:
```python
import functools

import jax
import jax.numpy as jnp
from jax import lax
from jax.experimental import pallas as pl
from jax.experimental.pallas import tpu as pltpu
from jax.sharding import PartitionSpec as P

MESH = pl.DeviceIdType.MESH
KINDS = 11
TO_PLANE, TO_X, TO_Y, FWD_Y, FWD_X, BACK_X, BACK_Y, OWN_X, OWN_Y, HOME, SHARE = range(KINDS)


def modulate(hidden, shift_row, scale_row):
    average = jnp.mean(hidden, axis=-1, keepdims=True)
    centred = hidden - average
    variance = jnp.mean(centred * centred, axis=-1, keepdims=True)
    return (centred * lax.rsqrt(variance + 1e-06) * (1.0 + scale_row) + shift_row).astype(
        jnp.bfloat16
    )


def plan(normed, routes, router, capacity, first, count):
    rows_count, width = normed.shape
    experts = router.shape[1]
    logits = jnp.dot(normed.astype(jnp.float32), router, precision=lax.Precision.HIGHEST)
    hits = routes[:, :, None] == jnp.arange(experts, dtype=jnp.int32)
    chosen = jnp.sum(jnp.where(hits, logits[:, None, :], 0.0), axis=-1)
    gate_sig = jax.nn.sigmoid(chosen)
    weights = gate_sig / jnp.sum(gate_sig, axis=-1, keepdims=True)
    named = jnp.any(hits, axis=1)
    earlier = lax.broadcasted_iota(jnp.int32, (rows_count, rows_count), 1) < (
        lax.broadcasted_iota(jnp.int32, (rows_count, rows_count), 0)
    )
    position = jnp.dot(
        earlier.astype(jnp.bfloat16),
        named.astype(jnp.bfloat16),
        preferred_element_type=jnp.float32,
    ).astype(jnp.int32)
    weight_of = jnp.sum(jnp.where(hits, weights[:, :, None], 0.0), axis=1)
    slots = jnp.arange(capacity, dtype=jnp.int32)
    combine_w = jnp.where(
        named[:, :, None] & (position[:, :, None] == slots), weight_of[:, :, None], 0.0
    )
    own_slots = first + jnp.arange(count, dtype=jnp.int32)
    dispatch = (named[:, :, None] & (position[:, :, None] == own_slots)).astype(jnp.bfloat16)
    gathered = jnp.einsum(
        "rs,rd->sd",
        dispatch.reshape(rows_count, experts * count),
        normed,
        preferred_element_type=jnp.float32,
    ).astype(jnp.bfloat16)
    return gathered.reshape(experts, count, width), combine_w


def layer_kernel(
    share,
    tok_ref,
    win_hbm,
    wout_hbm,
    out_ref,
    win,
    wout,
    rows,
    part,
    back_x,
    back_y,
    own_x,
    own_y,
    summed,
    home,
    other,
    w_sem,
    send_sem,
    recv_sem,
):
    experts, cap, width = tok_ref.shape
    half = width // 2
    quarters = lax.axis_size("expert") // experts
    me = lax.axis_index("expert")
    e_me, q_me = me // quarters, me % quarters
    qx, qy = q_me % 2, q_me // 2
    q_x = qy * 2 + (1 - qx)
    q_y = (1 - qy) * 2 + qx
    q_d = (1 - qy) * 2 + (1 - qx)
    dev_x = {"expert": e_me * quarters + q_x}
    dev_y = {"expert": e_me * quarters + q_y}
    sibling = {"step": 1 - lax.axis_index("step")}

    w_copies = [
        pltpu.make_async_copy(win_hbm, win, w_sem.at[0]),
        pltpu.make_async_copy(wout_hbm, wout, w_sem.at[1]),
    ]
    for copy in w_copies:
        copy.start()

    def column(e):
        return {"expert": e * quarters + q_me}

    def ahead(k):
        return (e_me + k) % experts

    def behind(k):
        return (e_me + experts - k) % experts

    barrier = pltpu.get_barrier_semaphore()
    peers = [dev_x, dev_y] + [column(ahead(k)) for k in range(1, experts)]
    if share:
        peers.append(sibling)
    for peer in peers:
        pl.semaphore_signal(barrier, inc=1, device_id=peer, device_id_type=MESH)
    pl.semaphore_wait(barrier, len(peers))

    started = []

    def send(kind, src, dst, device, sent, landed):
        copy = pltpu.make_async_remote_copy(
            src_ref=src,
            dst_ref=dst,
            send_sem=send_sem.at[kind, sent],
            recv_sem=recv_sem.at[kind, landed],
            device_id=device,
            device_id_type=MESH,
        )
        copy.start()
        started.append(copy)

    def arrived(kind, dst, landed):
        pltpu.make_async_remote_copy(
            src_ref=dst,
            dst_ref=dst,
            send_sem=send_sem.at[kind, landed],
            recv_sem=recv_sem.at[kind, landed],
            device_id=dev_x,
            device_id_type=MESH,
        ).wait_recv()

    def at(q):
        return pl.ds(pl.multiple_of(q * cap, cap), cap)

    left, right = pl.ds(0, half), pl.ds(half, half)

    for k in range(1, experts):
        to = ahead(k)
        send(TO_PLANE, tok_ref.at[to], rows.at[e_me, at(q_me)], column(to), to, e_me)
    rows[e_me, at(q_me), :] = tok_ref[e_me]

    def spread(k):
        j = behind(k)
        mine = rows.at[j, at(q_me)]
        if k > 0:
            arrived(TO_PLANE, mine, j)
        send(TO_X, mine, mine, dev_x, j, j)
        send(TO_Y, mine, mine, dev_y, j, j)

    def forward(k):
        j = behind(k)
        arrived(TO_X, rows.at[j, at(q_x)], j)
        block = rows.at[j, at(q_x), left]
        send(FWD_Y, block, block, dev_y, j, j)
        arrived(TO_Y, rows.at[j, at(q_y)], j)
        block = rows.at[j, at(q_y), right]
        send(FWD_X, block, block, dev_x, j, j)

    def compute(k):
        j = behind(k)
        arrived(FWD_Y, rows.at[j, at(q_d), left], j)
        arrived(FWD_X, rows.at[j, at(q_d), right], j)
        if k == 0:
            for copy in w_copies:
                copy.wait()
        hidden = jax.nn.gelu(
            jnp.dot(rows[j], win[...], preferred_element_type=jnp.float32), approximate=True
        ).astype(jnp.bfloat16)
        for columns in (left, right):
            part[j, :, columns] = jnp.dot(
                hidden, wout[:, columns], preferred_element_type=jnp.float32
            ).astype(jnp.bfloat16)
        send(BACK_X, part.at[j, at(q_d), left], back_x.at[j], dev_x, j, j)
        send(BACK_Y, part.at[j, at(q_d), right], back_y.at[j], dev_y, j, j)

    def gather(k):
        j = behind(k)
        arrived(BACK_X, back_x.at[j], j)
        part[j, at(q_y), left] = (
            part[j, at(q_y), left].astype(jnp.float32) + back_x[j].astype(jnp.float32)
        ).astype(jnp.bfloat16)
        send(OWN_Y, part.at[j, at(q_y)], own_y.at[j], dev_y, j, j)
        arrived(BACK_Y, back_y.at[j], j)
        part[j, at(q_x), right] = (
            part[j, at(q_x), right].astype(jnp.float32) + back_y[j].astype(jnp.float32)
        ).astype(jnp.bfloat16)
        send(OWN_X, part.at[j, at(q_x)], own_x.at[j], dev_x, j, j)

    def finish(k):
        j = behind(k)
        arrived(OWN_Y, own_y.at[j], j)
        arrived(OWN_X, own_x.at[j], j)
        total = (
            part[j, at(q_me), :].astype(jnp.float32)
            + own_x[j].astype(jnp.float32)
            + own_y[j].astype(jnp.float32)
        ).astype(jnp.bfloat16)
        if k == 0:
            home[j] = total
            if share:
                send(SHARE, home.at[j], other.at[j], sibling, j, j)
        else:
            summed[j] = total
            send(HOME, summed.at[j], home.at[e_me], column(j), j, e_me)

    stages = (spread, forward, compute, gather, finish)
    for turn in range(experts + len(stages) - 1):
        for lag, stage in enumerate(stages):
            if 0 <= turn - lag < experts:
                stage(turn - lag)

    for k in range(1, experts):
        j = ahead(k)
        arrived(HOME, home.at[j], j)
        if share:
            send(SHARE, home.at[j], other.at[j], sibling, j, j)
    if share:
        core = lax.axis_index("step")
        out_ref[core] = home[...]
        for j in range(experts):
            arrived(SHARE, other.at[j], j)
        out_ref[1 - core] = other[...]
    else:
        out_ref[0] = home[...]
    for copy in started:
        copy.wait_send()


def layer(tokens, weight_in, weight_out, share, collective_id):
    experts, cap, width = tokens.shape
    quarters = lax.axis_size("expert") // experts
    assert quarters == 4
    halves = 2 if share else 1
    bf16 = jnp.bfloat16
    vmem = pl.BlockSpec(memory_space=pltpu.VMEM)
    hbm = pl.BlockSpec(memory_space=pl.ANY)
    block = pltpu.VMEM((experts, cap, width), bf16)
    return pl.pallas_call(
        functools.partial(layer_kernel, share),
        out_shape=jax.ShapeDtypeStruct((halves, experts, cap, width), bf16),
        in_specs=[vmem, hbm, hbm],
        out_specs=vmem,
        scratch_shapes=[
            pltpu.VMEM(weight_in.shape, bf16),
            pltpu.VMEM(weight_out.shape, bf16),
            pltpu.VMEM((experts, quarters * cap, width), bf16),
            pltpu.VMEM((experts, quarters * cap, width), bf16),
            pltpu.VMEM((experts, cap, width // 2), bf16),
            pltpu.VMEM((experts, cap, width // 2), bf16),
            block,
            block,
            block,
            block,
            block,
            pltpu.SemaphoreType.DMA((2,)),
            pltpu.SemaphoreType.DMA((KINDS, experts)),
            pltpu.SemaphoreType.DMA((KINDS, experts)),
        ],
        compiler_params=pltpu.CompilerParams(
            collective_id=collective_id, has_side_effects=True, vmem_limit_bytes=48 * 1024 * 1024
        ),
    )(tokens, weight_in, weight_out)


def combine(returned, combine_w):
    halves, experts, cap, width = returned.shape
    rows_count = combine_w.shape[0]
    ordered = jnp.swapaxes(combine_w.reshape(rows_count, experts, halves, cap), 1, 2)
    return jnp.dot(
        ordered.reshape(rows_count, -1),
        returned.astype(jnp.float32).reshape(-1, width),
        precision=lax.Precision.HIGHEST,
        preferred_element_type=jnp.float32,
    )


def body(
    latents,
    modulation,
    shallow_routes,
    deep_routes,
    refresh,
    shallow_in,
    shallow_out,
    deep_in,
    deep_out,
    shallow_router,
    deep_router,
):
    experts = shallow_router.shape[1]
    rows_count = latents.shape[1]
    capacity = 2 * max(rows_count * 5 // 64, rows_count // experts)
    capacity = -(-capacity // 32) * 32
    step_idx = lax.axis_index("step")
    root_idx = refresh[0]
    own_mod = lax.dynamic_index_in_dim(modulation, step_idx, 0, keepdims=False)
    features = latents[0]
    normed = modulate(features, own_mod[0], own_mod[1])
    gathered, combine_w = plan(normed, shallow_routes[0], shallow_router, capacity, 0, capacity)
    returned = layer(gathered, shallow_in[0], shallow_out[0], False, 0)
    moe_shallow = combine(returned, combine_w)
    after_shallow = (features + own_mod[2] * moe_shallow).astype(jnp.bfloat16)
    normed_deep = modulate(after_shallow.astype(jnp.float32), own_mod[3], own_mod[4])
    from_other = lax.ppermute(normed_deep, "step", [(0, 1), (1, 0)])
    normed_root = jnp.where(root_idx == step_idx, normed_deep, from_other)
    part_cap = capacity // 2
    gathered_deep, combine_deep = plan(
        normed_root, deep_routes, deep_router, capacity, step_idx * part_cap, part_cap
    )
    returned_deep = layer(gathered_deep, deep_in[0], deep_out[0], True, 1)
    moe_deep = combine(returned_deep, combine_deep)
    root_gate = lax.dynamic_index_in_dim(modulation, root_idx, 0, keepdims=False)[5]
    deep_delta = (root_gate * moe_deep).astype(jnp.bfloat16)
    result = (after_shallow.astype(jnp.float32) + deep_delta.astype(jnp.float32)).astype(
        jnp.bfloat16
    )
    return result[None]


def solution(mesh):
    in_specs = (
        P("step", ("group", "expert"), None),
        P("group", None, None),
        P("step", ("group", "expert"), None),
        P(("group", "expert"), None),
        P(("group", "expert")),
        P("expert", None, None),
        P("expert", None, None),
        P("expert", None, None),
        P("expert", None, None),
        P(),
        P(),
    )
    out_specs = P("step", ("group", "expert"), None)
    return jax.shard_map(body, mesh=mesh, in_specs=in_specs, out_specs=out_specs, check_vma=False)
```

time: 377 us -> 130 us (0.34)
  blocking collectives: 164 us -> 0 us
  waiting for transfers between devices: 143 us -> 1.32 us
  Pallas kernels: 0 us -> 115 us
  matrix products: 27.2 us -> 5.05 us
  between operations: 14.3 us -> 1.03 us
  other arithmetic: 14.7 us -> 5.23 us
  starting transfers between devices: 9.3 us -> 0.07 us
    all_to_all x2 -> x0, blocking collectives: 164 us -> none  [the longest x1 84.7 us: body(): lax.all_to_all(spread(gathered_deep, slices), 'expert', split_axis=0, con...]
    all_to_all x2 -> x0, waiting for transfers between devices: 116 us -> none  [body(): lax.all_to_all(partial_value, 'expert', split_axis=0, concat_axis=0, tile...]
    pallas_call x0 -> x2, Pallas kernels: none -> 115 us  [layer(): pl.pallas_call(functools.partial(layer_kernel, share), out_shape=jax.Shap...]
    psum x1 -> x0, waiting for transfers between devices: 27.1 us -> none  [from_root(): return lax.psum(block, axis)]
    dot_general x6, matrix products: 26.3 us -> 3.02 us  [the longest x2 1.98 us: combine(): jnp.dot(ordered.reshape(rows_count, -1), returned.astype(jnp.float32).res...]
    all_to_all x2 -> x0, starting transfers between devices: 9.25 us -> none  [body(): lax.all_to_all(partial_value, 'expert', split_axis=0, concat_axis=0, tile...]
    reduce_sum x6 -> x2, other arithmetic: 5.25 us -> 0.03 us  [plan(): weight_of = jnp.sum(jnp.where(hits, weights[:, :, None], 0.0), axis=1)]
  transfers between devices with their start and end apart: 3 -> 1, of which waited for: 3 -> 1; matrix products, arithmetic and copies ran while one was open for 1% -> 0% of each run, Pallas kernels for 0% -> 0%
where the time goes in v1:
time: 130 us
  Pallas kernels  115 us (88%)
  other arithmetic  5.23 us (4%)
  matrix products  5.05 us (4%)
  local copies, waits for them, and re-layouts  2.4 us (2%)
  waiting for transfers between devices  1.32 us (1%)
    pallas_call x2, Pallas kernels, layer(): pl.pallas_call(functools.partial(layer_kernel, share), out_shape=jax.Shap...  115 us
  transfers between devices with their start and end apart: 1, of which 1 were waited for; matrix products, arithmetic and copies ran while one was open for 0% of the time, Pallas kernels for 0%

profile of v1, /device:TPU:0, one launch (start us, length us, event | category | flops | bytes accessed | tf_op | source)
XLA Modules:
  0.0 129.7 jit_solution(1140608559200680291)
XLA Ops:
  0.0 0.0 copy-start
  0.0 0.0 copy-start.4
  0.0 0.0 copy-start.8
  0.0 0.0 copy-start.1
  0.8 1.4 %reduce_sum.90 = f32[128]{0:T(128)S(1)} reduce(f32[1,128,1536]{2,1,0:T(8,128)} %param.11, f32[]{:T(128)} %constant.26.clone.1), dimensions={0,2}, to_apply=%region_1.2 | reduce | flops 196480 | bytes 786948 | tf_op jit(solution)/shard_map/reduce_sum | solution.py:16
  2.3 1.4 %multiply_reduce_fusion.1 = f32[128]{0:T(128)S(1)} fusion(f32[1,128,1536]{2,1,0:T(8,128)} %param.11, f32[128]{0:T(128)S(1)} %broadcast_multiply_fusion.1), kind=kLoop, calls=%fused_computation.20 | loop fusion | flops 589696 | bytes 787456 | tf_op jit(solution)/shard_map/reduce_sum | solution.py:18
  3.6 0.7 fusion.30
  4.3 0.9 dynamic-slice_reduce_fusion.1
  5.2 0.0 copy-done
  5.2 1.6 %fusion.15 = f32[128,4]{0,1:T(4,128)S(1)} fusion(f32[1536,4]{0,1:T(4,128)S(1)} %copy-done, f32[1,128,1536]{2,1,0:T(8,128)} %param.11, f32[1536]{0:T(1024)S(1)} %get-tuple-element.7, f32[1536]{0:T(1024)S(1)} %get-tuple-element.8, f32[128]{0:T(128)S(1)} %add_rsqrt_fusion.1, f32[128]{0:T(128)S(1)} %broadcast_multiply_fusion.1), kind=kOutput, calls=%fused_computation.27 | convolution fusion | flops 10420224 | bytes 826368 | tf_op jit(solution)/shard_map/dot_general | solution.py:27
  6.9 0.0 copy-done.8
  7.0 0.1 convolution_convert_fusion.3
  7.1 0.1 fusion.18
  7.2 0.0 copy-done.4
  7.2 0.5 convolution_convert_fusion
  7.7 0.0 copy-done.1
  7.7 73.3 %shard_map.109 = bf16[1,4,64,1536]{3,2,1,0:T(8,128)(2,1)S(1)} custom-call(bf16[4,64,1536]{2,1,0:T(8,128)(2,1)S(1)} %bitcast.59, bf16[1536,768]{1,0:T(8,128)(2,1)S(1)} %bitcast.61, bf16[768,1536]{1,0:T(8,128)(2,1)} %bitcast.65), custom_call_target="tpu_custom_call" | custom-call | tf_op jit(solution)/shard_map/pallas_call | solution.py:245
  81.0 0.0 copy-start.9
  81.0 0.0 copy-start.7
  81.0 0.6 fusion.32
  81.7 0.0 copy-start.5
  81.7 0.0 copy-start.2
  81.7 0.2 multiply_reduce_fusion
  81.9 0.6 copy-done.5
  82.6 0.2 add_convert_fusion
  82.8 0.1 collective-permute-start
  82.9 0.1 eq.128
  82.9 0.0 copy-done.9
  83.0 0.1 convolution_convert_fusion.2
  83.1 0.1 fusion.25
  83.2 1.3 %collective-permute-done = bf16[128,1536]{1,0:T(8,128)(2,1)S(1)} collective-permute-done((bf16[128,1536]{1,0:T(8,128)(2,1)S(1)}, bf16[128,1536]{1,0:T(8,128)(2,1)S(1)}, u32[]{:S(2)}, u32[]{:S(2)}) %collective-permute-start) | collective-permute-done | bytes 393248 | tf_op jit(solution)/shard_map/ppermute | solution.py:311
  84.5 0.0 copy-done.7
  84.5 0.4 fusion.16
  85.0 0.3 convolution_convert_fusion.1
  85.3 0.0 copy-done.2
  85.3 0.0 copy-start.3
  85.4 1.7 %copy-done.3 = bf16[1,768,1536]{2,1,0:T(8,128)(2,1)S(1)} copy-done((bf16[1,768,1536]{2,1,0:T(8,128)(2,1)S(1)}, bf16[1,768,1536]{2,1,0:T(8,128)(2,1)}, u32[]{:S(2)}) %copy-start.3) | copy-done | bytes 2359320
  87.0 0.0 copy-start.6
  87.0 41.3 %shard_map.110 = bf16[2,4,32,1536]{3,2,1,0:T(8,128)(2,1)S(1)} custom-call(bf16[4,32,1536]{2,1,0:T(8,128)(2,1)S(1)} %bitcast.64, bf16[1536,768]{1,0:T(8,128)(2,1)S(1)} %bitcast.62, bf16[768,1536]{1,0:T(8,128)(2,1)S(1)} %bitcast.63), custom_call_target="tpu_custom_call" | custom-call | tf_op jit(solution)/shard_map/pallas_call | solution.py:245
  128.3 0.0 copy-done.6
  128.3 1.3 %fusion.8 = bf16[1,128,1536]{2,1,0:T(8,128)(2,1)} fusion(f32[128,1536]{1,0:T(8,128)S(1)} %copy-done.6, bf16[2,4,32,1536]{3,2,1,0:T(8,128)(2,1)S(1)} %shard_map.110, f32[1536]{0:T(1024)S(1)} %get-tuple-element.5, f32[128,4]{0,1:T(4,128)S(1)} %select_reduce_fusion, s32[2,32]{1,0:T(2,128)S(1)} %multiply_add_fusion, ...), kind=kOutput, calls=%fused_computation.12 | convolution fusion | flops 605061120 | bytes 1977088 | tf_op jit(solution)/shard_map/dot_general | solution.py:276
  (17 shorter events, 0.3 us)
Async XLA Ops:
  0.0 5.2 %copy-start = (f32[1536,4]{0,1:T(4,128)S(1)}, f32[1536,4]{0,1:T(4,128)}, u32[]{:S(2)}) copy-start(f32[1536,4]{0,1:T(4,128)} %param.20) | copy-start | bytes 73732
  0.0 7.2 %copy-start.4 = (f32[1,128,1536]{2,1,0:T(8,128)S(1)}, f32[1,128,1536]{2,1,0:T(8,128)}, u32[]{:S(2)}) copy-start(f32[1,128,1536]{2,1,0:T(8,128)} %param.11) | copy-start | bytes 2359300
  0.0 6.9 %copy-start.8 = (s32[1,128,2]{1,2,0:T(2,128)S(1)}, s32[1,128,2]{1,2,0:T(2,128)}, u32[]{:S(2)}) copy-start(s32[1,128,2]{1,2,0:T(2,128)} %param.13) | copy-start | bytes 3076
  0.0 7.7 %copy-start.1 = (bf16[1,1536,768]{2,1,0:T(8,128)(2,1)S(1)}, bf16[1,1536,768]{2,1,0:T(8,128)(2,1)}, u32[]{:S(2)}) copy-start(bf16[1,1536,768]{2,1,0:T(8,128)(2,1)} %param.16) | copy-start | bytes 7077892
  81.0 1.9 %copy-start.9 = (s32[128,2]{0,1:T(2,128)S(1)}, s32[128,2]{0,1:T(2,128)}, u32[]{:S(2)}) copy-start(s32[128,2]{0,1:T(2,128)} %param.14) | copy-start | bytes 3076
  81.0 3.5 %copy-start.7 = (f32[1536,4]{0,1:T(4,128)S(1)}, f32[1536,4]{0,1:T(4,128)}, u32[]{:S(2)}) copy-start(f32[1536,4]{0,1:T(4,128)} %param.21) | copy-start | bytes 73732
  81.7 0.9 copy-start.5
  81.7 3.7 %copy-start.2 = (bf16[1,1536,768]{2,1,0:T(8,128)(2,1)S(1)}, bf16[1,1536,768]{2,1,0:T(8,128)(2,1)}, u32[]{:S(2)}) copy-start(bf16[1,1536,768]{2,1,0:T(8,128)(2,1)} %param.18) | copy-start | bytes 7077892
  82.8 1.8 %collective-permute-start = (bf16[128,1536]{1,0:T(8,128)(2,1)S(1)}, bf16[128,1536]{1,0:T(8,128)(2,1)S(1)}, u32[]{:S(2)}, u32[]{:S(2)}) collective-permute-start(bf16[128,1536]{1,0:T(8,128)(2,1)S(1)} %add_convert_fusion), channel_id=1, source_target_pairs={{0,1},{1,0},{2,3},{3,2},{4,5},{5,4},{6,7},{7,6},{8,9},{9,8},{10,11... | collective-permute-start | bytes 1179656 | tf_op jit(solution)/shard_map/ppermute | solution.py:311
  85.3 1.7 %copy-start.3 = (bf16[1,768,1536]{2,1,0:T(8,128)(2,1)S(1)}, bf16[1,768,1536]{2,1,0:T(8,128)(2,1)}, u32[]{:S(2)}) copy-start(bf16[1,768,1536]{2,1,0:T(8,128)(2,1)} %param.19) | copy-start | bytes 7077892
  87.0 41.3 %copy-start.6 = (f32[128,1536]{1,0:T(8,128)S(1)}, f32[128,1536]{1,0:T(8,128)}, u32[]{:S(2)}) copy-start(f32[128,1536]{1,0:T(8,128)} %copy-done.5) | copy-start | bytes 2359300

commit v2 on v1

--- a/solution.py
+++ b/solution.py
@@ -167,7 +167,7 @@
         j = behind(k)
         arrived(FWD_Y, rows.at[j, at(q_d), left], j)
         arrived(FWD_X, rows.at[j, at(q_d), right], j)
-        if k == 0:
+        if k == near_last[0]:
             for copy in w_copies:
                 copy.wait()
         hidden = jax.nn.gelu(
@@ -210,17 +210,27 @@
             summed[j] = total
             send(HOME, summed.at[j], home.at[e_me], column(j), j, e_me)
 
-    stages = (spread, forward, compute, gather, finish)
-    for turn in range(experts + len(stages) - 1):
-        for lag, stage in enumerate(stages):
-            if 0 <= turn - lag < experts:
-                stage(turn - lag)
-
-    for k in range(1, experts):
+    def relay(k):
         j = ahead(k)
         arrived(HOME, home.at[j], j)
         if share:
             send(SHARE, home.at[j], other.at[j], sibling, j, j)
+
+    near_first = list(range(experts))
+    near_last = near_first[1:] + [0]
+    stages = (
+        (spread, near_first),
+        (forward, near_first),
+        (compute, near_last),
+        (gather, near_last),
+        (finish, near_last),
+        (relay, near_last[:-1]),
+    )
+    for turn in range(experts + len(stages) - 1):
+        for lag, (stage, order) in enumerate(stages):
+            if 0 <= turn - lag < len(order):
+                stage(order[turn - lag])
+
     if share:
         core = lax.axis_index("step")
         out_ref[core] = home[...]

time: 130 us -> 132 us (1.015)
  Pallas kernels: 115 us -> 117 us
    pallas_call x2, Pallas kernels: 115 us -> 117 us  [layer(): pl.pallas_call(functools.partial(layer_kernel, share), out_shape=jax.Shap...]
where the time goes in v2:
time: 132 us
  Pallas kernels  117 us (89%)
  other arithmetic  5.23 us (4%)
  matrix products  5.04 us (4%)
  local copies, waits for them, and re-layouts  2.4 us (2%)
  waiting for transfers between devices  1.32 us (1%)
    pallas_call x2, Pallas kernels, layer(): pl.pallas_call(functools.partial(layer_kernel, share), out_shape=jax.Shap...  117 us
  transfers between devices with their start and end apart: 1, of which 1 were waited for; matrix products, arithmetic and copies ran while one was open for 0% of the time, Pallas kernels for 0%

profile of v2, /device:TPU:0, one launch (start us, length us, event | category | flops | bytes accessed | tf_op | source)
XLA Modules:
  0.0 132.0 jit_solution(484933387519190766)
XLA Ops:
  0.0 0.0 copy-start
  0.0 0.0 copy-start.4
  0.0 0.0 copy-start.8
  0.0 0.0 copy-start.1
  0.8 1.4 %reduce_sum.90 = f32[128]{0:T(128)S(1)} reduce(f32[1,128,1536]{2,1,0:T(8,128)} %param.11, f32[]{:T(128)} %constant.26.clone.1), dimensions={0,2}, to_apply=%region_1.2 | reduce | flops 196480 | bytes 786948 | tf_op jit(solution)/shard_map/reduce_sum | solution.py:16
  2.3 1.4 %multiply_reduce_fusion.1 = f32[128]{0:T(128)S(1)} fusion(f32[1,128,1536]{2,1,0:T(8,128)} %param.11, f32[128]{0:T(128)S(1)} %broadcast_multiply_fusion.1), kind=kLoop, calls=%fused_computation.20 | loop fusion | flops 589696 | bytes 787456 | tf_op jit(solution)/shard_map/reduce_sum | solution.py:18
  3.6 0.7 fusion.30
  4.3 0.9 dynamic-slice_reduce_fusion.1
  5.2 0.0 copy-done
  5.2 1.6 %fusion.15 = f32[128,4]{0,1:T(4,128)S(1)} fusion(f32[1536,4]{0,1:T(4,128)S(1)} %copy-done, f32[1,128,1536]{2,1,0:T(8,128)} %param.11, f32[1536]{0:T(1024)S(1)} %get-tuple-element.7, f32[1536]{0:T(1024)S(1)} %get-tuple-element.8, f32[128]{0:T(128)S(1)} %add_rsqrt_fusion.1, f32[128]{0:T(128)S(1)} %broadcast_multiply_fusion.1), kind=kOutput, calls=%fused_computation.27 | convolution fusion | flops 10420224 | bytes 826368 | tf_op jit(solution)/shard_map/dot_general | solution.py:27
  6.9 0.0 copy-done.8
  7.0 0.1 convolution_convert_fusion.3
  7.1 0.1 fusion.18
  7.2 0.0 copy-done.4
  7.2 0.5 convolution_convert_fusion
  7.7 0.0 copy-done.1
  7.7 74.0 %shard_map.109 = bf16[1,4,64,1536]{3,2,1,0:T(8,128)(2,1)S(1)} custom-call(bf16[4,64,1536]{2,1,0:T(8,128)(2,1)S(1)} %bitcast.59, bf16[1536,768]{1,0:T(8,128)(2,1)S(1)} %bitcast.61, bf16[768,1536]{1,0:T(8,128)(2,1)} %bitcast.65), custom_call_target="tpu_custom_call" | custom-call | tf_op jit(solution)/shard_map/pallas_call | solution.py:255
  81.7 0.0 copy-start.9
  81.8 0.0 copy-start.7
  81.8 0.6 fusion.32
  82.4 0.0 copy-start.5
  82.4 0.0 copy-start.2
  82.4 0.2 multiply_reduce_fusion
  82.7 0.6 copy-done.5
  83.3 0.2 add_convert_fusion
  83.5 0.1 collective-permute-start
  83.6 0.1 eq.128
  83.7 0.0 copy-done.9
  83.7 0.1 convolution_convert_fusion.2
  83.8 0.1 fusion.25
  84.0 1.3 collective-permute-done
  85.3 0.0 copy-done.7
  85.3 0.4 fusion.16
  85.8 0.3 convolution_convert_fusion.1
  86.1 0.0 copy-done.2
  86.1 0.0 copy-start.3
  86.1 1.7 %copy-done.3 = bf16[1,768,1536]{2,1,0:T(8,128)(2,1)S(1)} copy-done((bf16[1,768,1536]{2,1,0:T(8,128)(2,1)S(1)}, bf16[1,768,1536]{2,1,0:T(8,128)(2,1)}, u32[]{:S(2)}) %copy-start.3) | copy-done | bytes 2359320
  87.7 0.0 copy-start.6
  87.7 42.9 %shard_map.110 = bf16[2,4,32,1536]{3,2,1,0:T(8,128)(2,1)S(1)} custom-call(bf16[4,32,1536]{2,1,0:T(8,128)(2,1)S(1)} %bitcast.64, bf16[1536,768]{1,0:T(8,128)(2,1)S(1)} %bitcast.62, bf16[768,1536]{1,0:T(8,128)(2,1)S(1)} %bitcast.63), custom_call_target="tpu_custom_call" | custom-call | tf_op jit(solution)/shard_map/pallas_call | solution.py:255
  130.6 0.0 copy-done.6
  130.7 1.3 %fusion.8 = bf16[1,128,1536]{2,1,0:T(8,128)(2,1)} fusion(f32[128,1536]{1,0:T(8,128)S(1)} %copy-done.6, bf16[2,4,32,1536]{3,2,1,0:T(8,128)(2,1)S(1)} %shard_map.110, f32[1536]{0:T(1024)S(1)} %get-tuple-element.5, f32[128,4]{0,1:T(4,128)S(1)} %select_reduce_fusion, s32[2,32]{1,0:T(2,128)S(1)} %multiply_add_fusion, ...), kind=kOutput, calls=%fused_computation.12 | convolution fusion | flops 605061120 | bytes 1977088 | tf_op jit(solution)/shard_map/dot_general | solution.py:286
  (17 shorter events, 0.3 us)
Async XLA Ops:
  0.0 5.2 %copy-start = (f32[1536,4]{0,1:T(4,128)S(1)}, f32[1536,4]{0,1:T(4,128)}, u32[]{:S(2)}) copy-start(f32[1536,4]{0,1:T(4,128)} %param.20) | copy-start | bytes 73732
  0.0 7.2 %copy-start.4 = (f32[1,128,1536]{2,1,0:T(8,128)S(1)}, f32[1,128,1536]{2,1,0:T(8,128)}, u32[]{:S(2)}) copy-start(f32[1,128,1536]{2,1,0:T(8,128)} %param.11) | copy-start | bytes 2359300
  0.0 6.9 %copy-start.8 = (s32[1,128,2]{1,2,0:T(2,128)S(1)}, s32[1,128,2]{1,2,0:T(2,128)}, u32[]{:S(2)}) copy-start(s32[1,128,2]{1,2,0:T(2,128)} %param.13) | copy-start | bytes 3076
  0.0 7.7 %copy-start.1 = (bf16[1,1536,768]{2,1,0:T(8,128)(2,1)S(1)}, bf16[1,1536,768]{2,1,0:T(8,128)(2,1)}, u32[]{:S(2)}) copy-start(bf16[1,1536,768]{2,1,0:T(8,128)(2,1)} %param.16) | copy-start | bytes 7077892
  81.7 1.9 %copy-start.9 = (s32[128,2]{0,1:T(2,128)S(1)}, s32[128,2]{0,1:T(2,128)}, u32[]{:S(2)}) copy-start(s32[128,2]{0,1:T(2,128)} %param.14) | copy-start | bytes 3076
  81.8 3.5 %copy-start.7 = (f32[1536,4]{0,1:T(4,128)S(1)}, f32[1536,4]{0,1:T(4,128)}, u32[]{:S(2)}) copy-start(f32[1536,4]{0,1:T(4,128)} %param.21) | copy-start | bytes 73732
  82.4 0.9 copy-start.5
  82.4 3.7 %copy-start.2 = (bf16[1,1536,768]{2,1,0:T(8,128)(2,1)S(1)}, bf16[1,1536,768]{2,1,0:T(8,128)(2,1)}, u32[]{:S(2)}) copy-start(bf16[1,1536,768]{2,1,0:T(8,128)(2,1)} %param.18) | copy-start | bytes 7077892
  83.5 1.8 %collective-permute-start = (bf16[128,1536]{1,0:T(8,128)(2,1)S(1)}, bf16[128,1536]{1,0:T(8,128)(2,1)S(1)}, u32[]{:S(2)}, u32[]{:S(2)}) collective-permute-start(bf16[128,1536]{1,0:T(8,128)(2,1)S(1)} %add_convert_fusion), channel_id=1, source_target_pairs={{0,1},{1,0},{2,3},{3,2},{4,5},{5,4},{6,7},{7,6},{8,9},{9,8},{10,11... | collective-permute-start | bytes 1179656 | tf_op jit(solution)/shard_map/ppermute | solution.py:321
  86.1 1.7 %copy-start.3 = (bf16[1,768,1536]{2,1,0:T(8,128)(2,1)S(1)}, bf16[1,768,1536]{2,1,0:T(8,128)(2,1)}, u32[]{:S(2)}) copy-start(bf16[1,768,1536]{2,1,0:T(8,128)(2,1)} %param.19) | copy-start | bytes 7077892
  87.7 42.9 %copy-start.6 = (f32[128,1536]{1,0:T(8,128)S(1)}, f32[128,1536]{1,0:T(8,128)}, u32[]{:S(2)}) copy-start(f32[128,1536]{1,0:T(8,128)} %copy-done.5) | copy-start | bytes 2359300

commit v3 on v1

--- a/solution.py
+++ b/solution.py
@@ -210,17 +210,26 @@
             summed[j] = total
             send(HOME, summed.at[j], home.at[e_me], column(j), j, e_me)
 
-    stages = (spread, forward, compute, gather, finish)
-    for turn in range(experts + len(stages) - 1):
-        for lag, stage in enumerate(stages):
-            if 0 <= turn - lag < experts:
-                stage(turn - lag)
-
-    for k in range(1, experts):
+    def relay(k):
         j = ahead(k)
         arrived(HOME, home.at[j], j)
         if share:
             send(SHARE, home.at[j], other.at[j], sibling, j, j)
+
+    every = list(range(experts))
+    stages = (
+        (1, forward, every),
+        (0, spread, every),
+        (2, compute, every),
+        (3, gather, every),
+        (4, finish, every),
+        (6, relay, every[1:]),
+    )
+    for turn in range(experts + 5):
+        for lag, stage, order in stages:
+            if 0 <= turn - lag < len(order):
+                stage(order[turn - lag])
+
     if share:
         core = lax.axis_index("step")
         out_ref[core] = home[...]

time: 130 us -> 129 us (level)
  Pallas kernels: 115 us -> 113 us
    pallas_call x2, Pallas kernels: 115 us -> 113 us  [layer(): pl.pallas_call(functools.partial(layer_kernel, share), out_shape=jax.Shap...]
where the time goes in v3:
time: 129 us; the launch traced here: 128 us
  Pallas kernels  113 us (88%)
  other arithmetic  5.23 us (4%)
  matrix products  5.05 us (4%)
  local copies, waits for them, and re-layouts  2.4 us (2%)
  waiting for transfers between devices  1.32 us (1%)
    pallas_call x2, Pallas kernels, layer(): pl.pallas_call(functools.partial(layer_kernel, share), out_shape=jax.Shap...  113 us
  transfers between devices with their start and end apart: 1, of which 1 were waited for; matrix products, arithmetic and copies ran while one was open for 0% of the time, Pallas kernels for 0%

profile of v3, /device:TPU:0, one launch (start us, length us, event | category | flops | bytes accessed | tf_op | source)
XLA Modules:
  0.0 128.2 jit_solution(300868278626981628)
XLA Ops:
  0.0 0.0 copy-start
  0.0 0.0 copy-start.4
  0.0 0.0 copy-start.8
  0.0 0.0 copy-start.1
  0.8 1.4 %reduce_sum.90 = f32[128]{0:T(128)S(1)} reduce(f32[1,128,1536]{2,1,0:T(8,128)} %param.11, f32[]{:T(128)} %constant.26.clone.1), dimensions={0,2}, to_apply=%region_1.2 | reduce | flops 196480 | bytes 786948 | tf_op jit(solution)/shard_map/reduce_sum | solution.py:16
  2.3 1.4 %multiply_reduce_fusion.1 = f32[128]{0:T(128)S(1)} fusion(f32[1,128,1536]{2,1,0:T(8,128)} %param.11, f32[128]{0:T(128)S(1)} %broadcast_multiply_fusion.1), kind=kLoop, calls=%fused_computation.20 | loop fusion | flops 589696 | bytes 787456 | tf_op jit(solution)/shard_map/reduce_sum | solution.py:18
  3.6 0.7 fusion.30
  4.3 0.9 dynamic-slice_reduce_fusion.1
  5.2 0.0 copy-done
  5.2 1.6 %fusion.15 = f32[128,4]{0,1:T(4,128)S(1)} fusion(f32[1536,4]{0,1:T(4,128)S(1)} %copy-done, f32[1,128,1536]{2,1,0:T(8,128)} %param.11, f32[1536]{0:T(1024)S(1)} %get-tuple-element.7, f32[1536]{0:T(1024)S(1)} %get-tuple-element.8, f32[128]{0:T(128)S(1)} %add_rsqrt_fusion.1, f32[128]{0:T(128)S(1)} %broadcast_multiply_fusion.1), kind=kOutput, calls=%fused_computation.27 | convolution fusion | flops 10420224 | bytes 826368 | tf_op jit(solution)/shard_map/dot_general | solution.py:27
  6.9 0.0 copy-done.8
  7.0 0.1 convolution_convert_fusion.3
  7.1 0.1 fusion.18
  7.2 0.0 copy-done.4
  7.2 0.5 convolution_convert_fusion
  7.7 0.0 copy-done.1
  7.7 72.1 %shard_map.109 = bf16[1,4,64,1536]{3,2,1,0:T(8,128)(2,1)S(1)} custom-call(bf16[4,64,1536]{2,1,0:T(8,128)(2,1)S(1)} %bitcast.59, bf16[1536,768]{1,0:T(8,128)(2,1)S(1)} %bitcast.61, bf16[768,1536]{1,0:T(8,128)(2,1)} %bitcast.65), custom_call_target="tpu_custom_call" | custom-call | tf_op jit(solution)/shard_map/pallas_call | solution.py:254
  79.9 0.0 copy-start.9
  79.9 0.0 copy-start.7
  79.9 0.6 fusion.32
  80.5 0.0 copy-start.5
  80.5 0.0 copy-start.2
  80.6 0.2 multiply_reduce_fusion
  80.8 0.6 copy-done.5
  81.4 0.2 add_convert_fusion
  81.6 0.1 collective-permute-start
  81.7 0.1 eq.128
  81.8 0.0 copy-done.9
  81.8 0.1 convolution_convert_fusion.2
  82.0 0.1 fusion.25
  82.1 1.3 %collective-permute-done = bf16[128,1536]{1,0:T(8,128)(2,1)S(1)} collective-permute-done((bf16[128,1536]{1,0:T(8,128)(2,1)S(1)}, bf16[128,1536]{1,0:T(8,128)(2,1)S(1)}, u32[]{:S(2)}, u32[]{:S(2)}) %collective-permute-start) | collective-permute-done | bytes 393248 | tf_op jit(solution)/shard_map/ppermute | solution.py:320
  83.4 0.0 copy-done.7
  83.4 0.4 fusion.16
  83.9 0.3 convolution_convert_fusion.1
  84.2 0.0 copy-done.2
  84.2 0.0 copy-start.3
  84.2 1.7 %copy-done.3 = bf16[1,768,1536]{2,1,0:T(8,128)(2,1)S(1)} copy-done((bf16[1,768,1536]{2,1,0:T(8,128)(2,1)S(1)}, bf16[1,768,1536]{2,1,0:T(8,128)(2,1)}, u32[]{:S(2)}) %copy-start.3) | copy-done | bytes 2359320
  85.9 0.0 copy-start.6
  85.9 41.0 %shard_map.110 = bf16[2,4,32,1536]{3,2,1,0:T(8,128)(2,1)S(1)} custom-call(bf16[4,32,1536]{2,1,0:T(8,128)(2,1)S(1)} %bitcast.64, bf16[1536,768]{1,0:T(8,128)(2,1)S(1)} %bitcast.62, bf16[768,1536]{1,0:T(8,128)(2,1)S(1)} %bitcast.63), custom_call_target="tpu_custom_call" | custom-call | tf_op jit(solution)/shard_map/pallas_call | solution.py:254
  126.9 0.0 copy-done.6
  126.9 1.3 %fusion.8 = bf16[1,128,1536]{2,1,0:T(8,128)(2,1)} fusion(f32[128,1536]{1,0:T(8,128)S(1)} %copy-done.6, bf16[2,4,32,1536]{3,2,1,0:T(8,128)(2,1)S(1)} %shard_map.110, f32[1536]{0:T(1024)S(1)} %get-tuple-element.5, f32[128,4]{0,1:T(4,128)S(1)} %select_reduce_fusion, s32[2,32]{1,0:T(2,128)S(1)} %multiply_add_fusion, ...), kind=kOutput, calls=%fused_computation.12 | convolution fusion | flops 605061120 | bytes 1977088 | tf_op jit(solution)/shard_map/dot_general | solution.py:285
  (17 shorter events, 0.3 us)
Async XLA Ops:
  0.0 5.2 %copy-start = (f32[1536,4]{0,1:T(4,128)S(1)}, f32[1536,4]{0,1:T(4,128)}, u32[]{:S(2)}) copy-start(f32[1536,4]{0,1:T(4,128)} %param.20) | copy-start | bytes 73732
  0.0 7.2 %copy-start.4 = (f32[1,128,1536]{2,1,0:T(8,128)S(1)}, f32[1,128,1536]{2,1,0:T(8,128)}, u32[]{:S(2)}) copy-start(f32[1,128,1536]{2,1,0:T(8,128)} %param.11) | copy-start | bytes 2359300
  0.0 6.9 %copy-start.8 = (s32[1,128,2]{1,2,0:T(2,128)S(1)}, s32[1,128,2]{1,2,0:T(2,128)}, u32[]{:S(2)}) copy-start(s32[1,128,2]{1,2,0:T(2,128)} %param.13) | copy-start | bytes 3076
  0.0 7.7 %copy-start.1 = (bf16[1,1536,768]{2,1,0:T(8,128)(2,1)S(1)}, bf16[1,1536,768]{2,1,0:T(8,128)(2,1)}, u32[]{:S(2)}) copy-start(bf16[1,1536,768]{2,1,0:T(8,128)(2,1)} %param.16) | copy-start | bytes 7077892
  79.9 1.9 %copy-start.9 = (s32[128,2]{0,1:T(2,128)S(1)}, s32[128,2]{0,1:T(2,128)}, u32[]{:S(2)}) copy-start(s32[128,2]{0,1:T(2,128)} %param.14) | copy-start | bytes 3076
  79.9 3.5 %copy-start.7 = (f32[1536,4]{0,1:T(4,128)S(1)}, f32[1536,4]{0,1:T(4,128)}, u32[]{:S(2)}) copy-start(f32[1536,4]{0,1:T(4,128)} %param.21) | copy-start | bytes 73732
  80.5 0.9 copy-start.5
  80.5 3.7 %copy-start.2 = (bf16[1,1536,768]{2,1,0:T(8,128)(2,1)S(1)}, bf16[1,1536,768]{2,1,0:T(8,128)(2,1)}, u32[]{:S(2)}) copy-start(bf16[1,1536,768]{2,1,0:T(8,128)(2,1)} %param.18) | copy-start | bytes 7077892
  81.6 1.8 %collective-permute-start = (bf16[128,1536]{1,0:T(8,128)(2,1)S(1)}, bf16[128,1536]{1,0:T(8,128)(2,1)S(1)}, u32[]{:S(2)}, u32[]{:S(2)}) collective-permute-start(bf16[128,1536]{1,0:T(8,128)(2,1)S(1)} %add_convert_fusion), channel_id=1, source_target_pairs={{0,1},{1,0},{2,3},{3,2},{4,5},{5,4},{6,7},{7,6},{8,9},{9,8},{10,11... | collective-permute-start | bytes 1179656 | tf_op jit(solution)/shard_map/ppermute | solution.py:320
  84.2 1.7 %copy-start.3 = (bf16[1,768,1536]{2,1,0:T(8,128)(2,1)S(1)}, bf16[1,768,1536]{2,1,0:T(8,128)(2,1)}, u32[]{:S(2)}) copy-start(bf16[1,768,1536]{2,1,0:T(8,128)(2,1)} %param.19) | copy-start | bytes 7077892
  85.9 41.0 %copy-start.6 = (f32[128,1536]{1,0:T(8,128)S(1)}, f32[128,1536]{1,0:T(8,128)}, u32[]{:S(2)}) copy-start(f32[128,1536]{1,0:T(8,128)} %copy-done.5) | copy-start | bytes 2359300
